TPU v7x, 32 devices: a whole 2x2x4 slice. The times are simulated.
32 devices in a mesh: dp: 8 (over z, x), expert: 4 (over y, core).
Axes of the slice: x: 2, y: 2, z: 4, core: 2. Of those that a mesh axis runs over, the one named last changes fastest.
Arguments:
- layer_in: bfloat16 [8192, 1024], P(('dp', 'expert')), may hold values from -6 to 6
- body_of: int32 [8192], P(('dp', 'expert')), may hold values from 0 to 5, as said below
- expert_of: int32 [8192, 1], P(('dp', 'expert')), may hold values from 0 to 7; in each aligned block of 256 rows (0 to 255, 256 to 511, ...) at most 48 rows name the same one
- w_qkv: bfloat16 [1024, 1536], replicated, may hold values from -0.1875 to 0.1875
- w_o: bfloat16 [1024, 512], replicated, may hold values from -0.25 to 0.25
- w_up: bfloat16 [8, 1024, 1024], P('expert', None, 'dp'), may hold values from -0.1875 to 0.1875
- w_down: bfloat16 [8, 1024, 1024], P('expert', 'dp'), may hold values from -0.1875 to 0.1875
- d_out: bfloat16 [8192, 1024], P(('dp', 'expert')), may hold values from -6 to 6
Outputs:
- out: bfloat16 [8192, 1024], P(('dp', 'expert'))
- grad_input: bfloat16 [8192, 1024], P(('dp', 'expert'))
- grad_qkv: float32 [1024, 1536], P(('dp', 'expert'))
- grad_o: float32 [1024, 512], P(('dp', 'expert'))
- grad_up: float32 [8, 1024, 1024], P('expert', None, 'dp')
- grad_down: float32 [8, 1024, 1024], P('expert', 'dp')
Inputs may be any that keep to these rules, and one draw needn't show every extreme that they name: `body_of`: within each device's 256 rows the ids start at 0 and rise by one at each new body; every body has 16 to 128 tokens, no body crosses a multiple of 128 rows of its device, no block of 128 rows holds more than 3 bodies, and some device holds 3 bodies in each of its blocks. `expert_of`: in the 256 rows of one device no expert is named more than 48 times, a bound that some block reaches.
All inputs are finite; a program needn't handle non-finite values.
Results may differ from a plain program's by a relative error of at most 0.014.
Values may be sent and summed in bfloat16 or wider, within the bound.
A program may use at most 128 MiB of HBM per device.

v0:
```python
import jax
import jax.numpy as jnp
from jax import lax
from jax.sharding import PartitionSpec as P

HD = 64
EPSILON = 1e-06


def rms_norm(values):
    scale = lax.rsqrt(jnp.mean(values * values, axis=-1, keepdims=True) + EPSILON)
    return (values * scale).astype(jnp.bfloat16)


def gelu_tanh(values):
    return jax.nn.gelu(values, approximate=True)


def gelu_back(pre_act, cotangent):
    return jax.vjp(gelu_tanh, pre_act)[1](cotangent)[0]


def row_contract(left, right):
    return lax.dot_general(
        left, right, (((0,), (0,)), ((), ())), preferred_element_type=jnp.float32
    )


def col_contract(left, right):
    return lax.dot_general(
        left, right, (((1,), (1,)), ((), ())), preferred_element_type=jnp.float32
    )


def attention_core(packed, labels_row):
    rows = packed.shape[0]
    blocks = rows // 128
    width = packed.shape[1] // 3
    heads = width // HD
    parts = packed.reshape(blocks, 128, 3, heads, HD)
    query = parts[:, :, 0]
    keys = parts[:, :, 1]
    values = parts[:, :, 2]
    scores = jnp.einsum(
        "bqhc,bkhc->bhqk", query, keys, preferred_element_type=jnp.float32
    ) * HD ** (-0.5)
    labels = labels_row.reshape(blocks, 128)
    same = (labels[:, :, None] == labels[:, None, :])[:, None]
    weights = jnp.where(same, jnp.exp(scores), 0.0)
    probs = (weights / jnp.sum(weights, axis=-1, keepdims=True)).astype(jnp.bfloat16)
    mixed = jnp.einsum("bhqk,bkhc->bqhc", probs, values, preferred_element_type=jnp.float32)
    return mixed.astype(jnp.bfloat16).reshape(rows, width)


def stage_perm(count, bit):
    return [(i, i ^ bit) for i in range(count)]


def halve(values, axis_name, count, axis, bit):
    own = lax.axis_index(axis_name) // bit % 2
    keep = lax.dynamic_index_in_dim(values, own, axis, keepdims=False)
    give = lax.dynamic_index_in_dim(values, 1 - own, axis, keepdims=False).astype(jnp.bfloat16)
    came = lax.ppermute(give, axis_name, stage_perm(count, bit))
    return keep + came.astype(jnp.float32)


def scatter_sum(term):
    groups, shards = (lax.axis_size("dp"), lax.axis_size("expert"))
    rows, cols = term.shape
    own_rows = rows // (groups * shards)
    left = shards
    value = term.reshape(groups * shards * own_rows, cols)
    lead = groups
    bit = 1
    while bit < shards:
        left //= 2
        value = halve(value.reshape(lead, left, 2, own_rows, cols), "expert", shards, 2, bit)
        bit *= 2
    left = groups
    bit = 1
    while bit < groups:
        left //= 2
        value = halve(value.reshape(left, 2, own_rows, cols), "dp", groups, 1, bit)
        bit *= 2
    return value.reshape(own_rows, cols)


def ring_pairs(groups, step):
    half = groups // 2
    return [(i, (i // 2 + step) % half * 2 + i % 2) for i in range(groups)]


def ring_gather(shard, pairs, count):
    slots = [shard]
    for _ in range(count - 1):
        slots.append(lax.ppermute(slots[-1], "dp", pairs))
    return slots


def ring_reduce(slots, pairs):
    count = len(slots)
    total = slots[1 % count]
    for step in range(count - 1):
        came = lax.ppermute(total.astype(jnp.bfloat16), "dp", pairs)
        total = came.astype(jnp.float32) + slots[(step + 2) % count]
    return total


def on_device(layer_in, body_of, expert_of, w_qkv, w_o, w_up, w_down, d_out):
    tok_rows = layer_in.shape[0]
    width = layer_in.shape[1]
    shards = lax.axis_size("expert")
    groups = lax.axis_size("dp")
    half = groups // 2
    local_experts = w_up.shape[0]
    all_experts = local_experts * shards
    capacity = 3 * tok_rows // (2 * all_experts)
    received = shards * capacity
    partner = stage_perm(groups, 1)
    forth, back = (ring_pairs(groups, 1), ring_pairs(groups, -1))
    full_up = jnp.concatenate(ring_gather(w_up, forth, half), axis=2)
    full_down = jnp.concatenate(ring_gather(w_down, forth, half), axis=1)
    ids = expert_of[:, 0]
    at = jnp.arange(tok_rows, dtype=jnp.int32)
    earlier = (ids[:, None] == ids[None, :]) & (at[None, :] < at[:, None])
    ranks = jnp.sum(earlier.astype(jnp.int32), axis=1)
    slots = ids * capacity + ranks
    places = jnp.arange(all_experts * capacity, dtype=jnp.int32)
    spread = (places[:, None] == slots[None, :]).astype(jnp.bfloat16)

    def to_experts(values):
        store = jnp.dot(spread, values, preferred_element_type=jnp.float32).astype(jnp.bfloat16)
        store = store.reshape(shards, local_experts, capacity, width)
        sent = lax.all_to_all(store, "expert", split_axis=0, concat_axis=2, tiled=True)
        own = sent.reshape(local_experts, received, width)
        return jnp.concatenate([own, lax.ppermute(own, "dp", partner)], axis=1)

    def to_tokens(values):
        other = lax.ppermute(values[:, received:].astype(jnp.bfloat16), "dp", partner)
        total = (values[:, :received] + other.astype(jnp.float32)).astype(jnp.bfloat16)
        total = total.reshape(local_experts, shards, capacity, width)
        returned = lax.all_to_all(total, "expert", split_axis=1, concat_axis=0, tiled=True)
        returned = returned.reshape(all_experts * capacity, width)
        return row_contract(spread, returned)

    grads_in = to_experts(d_out)
    layer_f = layer_in.astype(jnp.float32)
    normed, norm_x_back = jax.vjp(rms_norm, layer_f)
    packed = jnp.dot(normed, w_qkv, preferred_element_type=jnp.float32).astype(jnp.bfloat16)
    mixed, core_back = jax.vjp(lambda value: attention_core(value, body_of), packed)
    resid = (layer_f + col_contract(mixed, w_o)).astype(jnp.bfloat16)
    inner, norm_h_back = jax.vjp(rms_norm, resid.astype(jnp.float32))
    inputs = to_experts(inner)
    d_hidden = jnp.einsum("esd,efd->esf", grads_in, full_down, preferred_element_type=jnp.float32)
    pre_act = jnp.einsum("esd,edf->esf", inputs, full_up, preferred_element_type=jnp.float32)
    hidden = gelu_tanh(pre_act).astype(jnp.bfloat16)
    d_pre = gelu_back(pre_act, d_hidden).astype(jnp.bfloat16)
    d_inputs = jnp.einsum("esf,edf->esd", d_pre, full_up, preferred_element_type=jnp.float32)
    d_inner = to_tokens(d_inputs).astype(jnp.bfloat16)
    part_up = jnp.einsum("esd,esf->edf", inputs, d_pre, preferred_element_type=jnp.float32)
    part_down = jnp.einsum("esf,esd->efd", hidden, grads_in, preferred_element_type=jnp.float32)
    grad_up = ring_reduce(jnp.split(part_up, half, axis=2), forth)
    grad_down = ring_reduce(jnp.split(part_down, half, axis=1), forth)
    result = jnp.einsum("esf,efd->esd", hidden, full_down, preferred_element_type=jnp.float32)
    expert_out = to_tokens(result)
    out = (resid.astype(jnp.float32) + expert_out).astype(jnp.bfloat16)
    d_resid = (d_out.astype(jnp.float32) + norm_h_back(d_inner)[0]).astype(jnp.bfloat16)
    grad_o = scatter_sum(row_contract(d_resid, mixed))
    d_mixed = jnp.dot(d_resid, w_o, preferred_element_type=jnp.float32).astype(jnp.bfloat16)
    d_packed = core_back(d_mixed)[0]
    grad_qkv = scatter_sum(row_contract(normed, d_packed))
    d_normed = col_contract(d_packed, w_qkv).astype(jnp.bfloat16)
    grad_input = (d_resid.astype(jnp.float32) + norm_x_back(d_normed)[0]).astype(jnp.bfloat16)
    return (out, grad_input, grad_qkv, grad_o, grad_up, grad_down)


def solution(mesh):
    in_specs = (
        P(("dp", "expert"), None),
        P(("dp", "expert")),
        P(("dp", "expert"), None),
        P(),
        P(),
        P("expert", None, "dp"),
        P("expert", "dp", None),
        P(("dp", "expert"), None),
    )
    out_specs = (
        P(("dp", "expert"), None),
        P(("dp", "expert"), None),
        P(("dp", "expert"), None),
        P(("dp", "expert"), None),
        P("expert", None, "dp"),
        P("expert", "dp", None),
    )
    return jax.shard_map(
        on_device, mesh=mesh, in_specs=in_specs, out_specs=out_specs, check_vma=False
    )
```

profile of v0, /device:TPU:0, one launch (start us, length us, event | category | flops | bytes accessed | tf_op | source)
XLA Modules:
  0.0 248.4 jit_solution(4098963044247727574)
XLA Ops:
  0.6 3.1 %collective-permute-start.1 = (bf16[2,1024,128]{2,1,0:T(8,128)(2,1)}, bf16[2,1024,128]{2,1,0:T(8,128)(2,1)}, u32[]{:S(2)}, u32[]{:S(2)}) collective-permute-start(bf16[2,1024,128]{2,1,0:T(8,128)(2,1)} %param.13), channel_id=1, source_target_pairs={{0,8},{4,12},{8,16},{12,20},{16,24},{20,28},{24,0},{28,4},{1,9},{5... | collective-permute-start | bytes 1572872 | tf_op jit(solution)/shard_map/ppermute | solution.py:96
  3.7 1.6 collective-permute-start.4
  9.0 3.0 %convolution_convert_fusion = bf16[256,1536]{1,0:T(8,128)(2,1)} fusion(bf16[1024,1536]{1,0:T(8,128)(2,1)S(1)} %copy-done, bf16[256,1024]{1,0:T(8,128)(2,1)} %param.8, f32[256]{0:T(256)S(1)} %fusion.71), kind=kOutput, calls=%fused_computation.2 | convolution fusion | flops 806486016 | bytes 4457472 | tf_op jit(solution)/shard_map/dot_general | solution.py:149
  12.0 3.1 %reshape.185 = bf16[2,128,3,8,64]{4,3,2,1,0:T(8,128)(2,1)} reshape(bf16[256,1536]{1,0:T(8,128)(2,1)} %convolution_convert_fusion) | data formatting | bytes 1572864 | tf_op jit(solution)/shard_map/jvp()/reshape | solution.py:40
  15.1 2.5 %fusion.80 = (bf16[2,128,1,8,64]{4,3,2,1,0:T(8,128)(2,1)}, bf16[2,128,1,8,64]{4,3,2,1,0:T(8,128)(2,1)}, bf16[2,128,1,8,64]{4,3,2,1,0:T(8,128)(2,1)}) fusion(bf16[2,128,3,8,64]{4,3,2,1,0:T(8,128)(2,1)} %reshape.185), kind=kLoop, calls=%fused_computation.164 | loop fusion | bytes 1572864 | tf_op jit(solution)/shard_map/jvp()/slice | solution.py:43
  18.9 2.0 copy.91
  21.0 2.0 copy.92
  29.1 4.2 %all-to-all-start = ((bf16[4,2,48,1024]{3,2,1,0:T(8,128)(2,1)}), bf16[4,2,48,1024]{3,2,1,0:T(8,128)(2,1)}, u32[]{:S(2)}, u32[]{:S(2)}) async-start(bf16[4,2,48,1024]{3,2,1,0:T(8,128)(2,1)} %bitcast.159), calls=%async_computation | async-start | bytes 1572864 | tf_op jit(solution)/shard_map/all_to_all | solution.py:134
  33.4 1.6 collective-permute-start.2
  35.1 2.3 convolution_convert_fusion.1
  37.4 7.7 %all-to-all-done = bf16[4,2,48,1024]{3,2,1,0:T(8,128)(2,1)} async-done(((bf16[4,2,48,1024]{3,2,1,0:T(8,128)(2,1)}), bf16[4,2,48,1024]{3,2,1,0:T(8,128)(2,1)}, u32[]{:S(2)}, u32[]{:S(2)}) %all-to-all-start) | async-done | bytes 786464 | tf_op jit(solution)/shard_map/all_to_all | solution.py:134
  45.1 4.2 %all-to-all-start.2 = ((bf16[4,2,48,1024]{3,2,1,0:T(8,128)(2,1)}), bf16[4,2,48,1024]{3,2,1,0:T(8,128)(2,1)}, u32[]{:S(2)}, u32[]{:S(2)}) async-start(bf16[4,2,48,1024]{3,2,1,0:T(8,128)(2,1)} %bitcast.158), calls=%async_computation.2 | async-start | bytes 1572864 | tf_op jit(solution)/shard_map/all_to_all | solution.py:134
  49.3 2.0 constant_dynamic-update-slice_fusion.3
  51.2 2.1 copy.59
  54.8 1.6 collective-permute-start.3
  57.2 4.3 %collective-permute-done.5 = bf16[2,128,1024]{2,1,0:T(8,128)(2,1)} collective-permute-done((bf16[2,128,1024]{2,1,0:T(8,128)(2,1)}, bf16[2,128,1024]{2,1,0:T(8,128)(2,1)}, u32[]{:S(2)}, u32[]{:S(2)}) %collective-permute-start.5) | collective-permute-done | bytes 524320 | tf_op jit(solution)/shard_map/ppermute | solution.py:96
  61.5 1.9 constant_dynamic-update-slice_fusion.2
  63.4 1.9 constant_dynamic-update-slice_fusion.6
  68.1 1.9 constant_dynamic-update-slice_fusion.1
  70.0 1.9 constant_dynamic-update-slice_fusion.5
  72.7 1.9 constant_dynamic-update-slice_fusion
  74.6 8.8 %collective-permute-done.6 = bf16[2,128,1024]{2,1,0:T(8,128)(2,1)} collective-permute-done((bf16[2,128,1024]{2,1,0:T(8,128)(2,1)}, bf16[2,128,1024]{2,1,0:T(8,128)(2,1)}, u32[]{:S(2)}, u32[]{:S(2)}) %collective-permute-start.6) | collective-permute-done | bytes 524320 | tf_op jit(solution)/shard_map/ppermute | solution.py:96
  83.5 1.9 constant_dynamic-update-slice_fusion.4
  85.4 3.0 %fusion.40 = f32[2,384,512]{2,1,0:T(8,128)S(1)} fusion(bf16[2,1024,512]{2,1,0:T(8,128)(2,1)} %constant_dynamic-update-slice_fusion, bf16[2,192,1024]{2,1,0:T(8,128)(2,1)} %collective-permute-done, bf16[2,192,1024]{2,1,0:T(8,128)(2,1)} %bitcast.9), kind=kOutput, calls=%fused_computation.92 | convolution fusion | flops 808452096 | bytes 5242880 | tf_op jit(solution)/shard_map/esd,edf->esf/dot_general | solution.py:155
  88.5 1.8 collective-permute-done.8
  90.3 3.7 %fusion.6 = bf16[2,384,512]{2,1,0:T(8,128)(2,1)S(1)} fusion(f32[2,384,512]{2,1,0:T(8,128)S(1)} %fusion.40, bf16[2,512,1024]{2,1,0:T(8,128)(2,1)} %constant_dynamic-update-slice_fusion.4, bf16[2,192,1024]{2,1,0:T(8,128)(2,1)S(1)} %collective-permute-done.8, bf16[2,192,1024]{2,1,0:T(8,128)(2,1)S(1)} %bitcast.175), kind=kOutput, calls=%fused_computation.21 | convolution fusion | flops 816316416 | bytes 6029312 | tf_op jit(solution)/shard_map/esd,efd->esf/dot_general | solution.py:154
  94.0 2.9 %fusion.81 = f32[2,384,1024]{2,1,0:T(8,128)S(1)} fusion(bf16[2,384,512]{2,1,0:T(8,128)(2,1)S(1)} %fusion.6, bf16[2,1024,512]{2,1,0:T(8,128)(2,1)} %constant_dynamic-update-slice_fusion), kind=kOutput, calls=%fused_computation.165 | convolution fusion | flops 805306368 | bytes 6029312 | tf_op jit(solution)/shard_map/esf,edf->esd/dot_general | solution.py:158
  96.9 1.7 copy-done.3
  101.1 3.3 %fusion.79 = f32[2,384,1024]{2,1,0:T(8,128)S(1)} fusion(bf16[2,512,1024]{2,1,0:T(8,128)(2,1)} %constant_dynamic-update-slice_fusion.4, f32[2,384,512]{2,1,0:T(8,128)} %copy-done.22), kind=kOutput, calls=%fused_computation.163 | convolution fusion | flops 808845312 | bytes 6815744 | tf_op jit(solution)/shard_map/esf,efd->esd/dot_general | solution.py:164
  109.3 1.6 collective-permute-start.23
  110.9 9.4 %collective-permute-done.9 = bf16[2,192,1024]{2,1,0:T(8,128)(2,1)} collective-permute-done((bf16[2,192,1024]{2,1,0:T(8,128)(2,1)}, bf16[2,192,1024]{2,1,0:T(8,128)(2,1)}, u32[]{:S(2)}, u32[]{:S(2)}) %collective-permute-start.9) | collective-permute-done | bytes 786464 | tf_op jit(solution)/shard_map/ppermute | solution.py:139
  122.7 4.2 %all-to-all-start.3 = ((bf16[2,4,48,1024]{3,2,0,1:T(8,128)(2,1)}), bf16[2,4,48,1024]{3,2,0,1:T(8,128)(2,1)}, u32[]{:S(2)}, u32[]{:S(2)}) async-start(bf16[2,4,48,1024]{3,2,0,1:T(8,128)(2,1)} %copy.62), calls=%async_computation.3 | async-start | bytes 1572864 | tf_op jit(solution)/shard_map/all_to_all | solution.py:142
  126.9 2.9 %fusion.39 = f32[2,1024,512]{2,1,0:T(8,128)S(1)} fusion(bf16[2,384,512]{2,1,0:T(8,128)(2,1)} %copy-done.18, bf16[2,192,1024]{2,1,0:T(8,128)(2,1)} %collective-permute-done, bf16[2,192,1024]{2,1,0:T(8,128)(2,1)} %bitcast.9), kind=kOutput, calls=%fused_computation.91 | convolution fusion | flops 808452096 | bytes 6553600 | tf_op jit(solution)/shard_map/esd,esf->edf/dot_general | solution.py:160
  129.8 2.0 copy-done.2
  132.9 1.6 collective-permute-start.20
  134.5 2.3 fusion.34
  136.9 1.8 all-to-all-done.3
  138.7 2.0 fusion.32
  143.0 1.8 copy.63
  144.8 1.7 reshape.175
  146.5 1.7 fusion.14
  148.1 1.7 fusion.22
  155.0 2.0 copy.70
  157.0 2.3 fusion.42
  159.3 2.7 %copy-done.1 = f32[8,2,2,32,1536]{4,3,2,1,0:T(8,128)} copy-done((f32[8,2,2,32,1536]{4,3,2,1,0:T(8,128)}, f32[8,2,2,32,1536]{4,3,2,1,0:T(8,128)S(1)}, u32[]{:S(2)}) %copy-start.1) | copy-done | bytes 6291480
  163.4 2.5 fusion.36
  165.9 1.6 collective-permute-start.21
  169.8 4.2 %all-to-all-start.1 = ((bf16[2,4,48,1024]{3,2,0,1:T(8,128)(2,1)}), bf16[2,4,48,1024]{3,2,0,1:T(8,128)(2,1)}, u32[]{:S(2)}, u32[]{:S(2)}) async-start(bf16[2,4,48,1024]{3,2,0,1:T(8,128)(2,1)} %copy.60), calls=%async_computation.1 | async-start | bytes 1572864 | tf_op jit(solution)/shard_map/all_to_all | solution.py:142
  174.0 2.3 fusion.33
  176.4 6.3 %collective-permute-done.21 = bf16[2,1024,128]{2,1,0:T(8,128)(2,1)} collective-permute-done((bf16[2,1024,128]{2,1,0:T(8,128)(2,1)}, bf16[2,1024,128]{2,1,0:T(8,128)(2,1)}, u32[]{:S(2)}, u32[]{:S(2)}) %collective-permute-start.21) | collective-permute-done | bytes 524320 | tf_op jit(solution)/shard_map/ppermute | solution.py:104
  182.7 2.3 fusion.35
  185.0 2.1 copy.73
  190.8 2.6 %fusion.11 = bf16[256,1024]{1,0:T(8,128)(2,1)} fusion(bf16[384,1024]{1,0:T(8,128)(2,1)} %bitcast.13, bf16[256,1024]{1,0:T(8,128)(2,1)} %copy-done.7, s32[256]{0:T(256)S(1)} %multiply_add_fusion.1), kind=kOutput, calls=%fused_computation.45 | convolution fusion | flops 202211328 | bytes 1836032 | tf_op jit(solution)/shard_map/dot_general | solution.py:24
  193.4 3.0 %bitcast_add_fusion = f32[8,2,32,1536]{3,2,1,0:T(8,128)S(1)} fusion(bf16[8,2,32,1536]{3,2,1,0:T(8,128)(2,1)} %collective-permute-done.10, f32[8,2,2,32,1536]{4,3,2,1,0:T(8,128)} %copy-done.1, s32[]{:T(128)S(6)} %select_n.111), kind=kLoop, calls=%fused_computation | loop fusion | flops 1572864 | bytes 7864324 | tf_op jit(solution)/shard_map/add | solution.py:64
  198.0 1.9 collective-permute-start.16
  199.9 2.5 %slice_add_fusion.2 = f32[2,128,1024]{2,1,0:T(8,128)} fusion(f32[2,512,1024]{2,1,0:T(8,128)} %copy-done.16, bf16[2,128,1024]{2,1,0:T(8,128)(2,1)} %collective-permute-done.25), kind=kLoop, calls=%fused_computation.74 | loop fusion | flops 524288 | bytes 2621440 | tf_op jit(solution)/shard_map/add | solution.py:105
  202.4 19.7 %collective-permute-done.16 = bf16[8,1,32,512]{3,2,1,0:T(8,128)(2,1)S(1)} collective-permute-done((bf16[8,1,32,512]{3,2,1,0:T(8,128)(2,1)S(1)}, bf16[8,1,32,512]{3,2,1,0:T(8,128)(2,1)S(1)}, u32[]{:S(2)}, u32[]{:S(2)}) %collective-permute-start.16) | collective-permute-done | bytes 262176 | tf_op jit(solution)/shard_map/ppermute | solution.py:63
  222.2 1.6 collective-permute-start.17
  224.7 2.4 slice_add_fusion.5
  227.1 1.6 collective-permute-done.17
  228.8 7.0 %collective-permute-done.12 = bf16[4,32,1536]{2,1,0:T(8,128)(2,1)S(1)} collective-permute-done((bf16[4,32,1536]{2,1,0:T(8,128)(2,1)S(1)}, bf16[4,32,1536]{2,1,0:T(8,128)(2,1)S(1)}, u32[]{:S(2)}, u32[]{:S(2)}) %collective-permute-start.12) | collective-permute-done | bytes 393248 | tf_op jit(solution)/shard_map/ppermute | solution.py:63
  236.1 4.4 %collective-permute-start.19 = (bf16[1,32,512]{2,1,0:T(8,128)(2,1)S(1)}, bf16[1,32,512]{2,1,0:T(8,128)(2,1)S(1)}, u32[]{:S(2)}, u32[]{:S(2)}) collective-permute-start(bf16[1,32,512]{2,1,0:T(8,128)(2,1)S(1)} %dynamic-slice_convert_fusion.7), channel_id=1, source_target_pairs={{0,16},{4,20},{8,24},{12,28},{16,0},{20,4},{24,8},{28,12},{1,17},{... | collective-permute-start | bytes 98312 | tf_op jit(solution)/shard_map/ppermute | solution.py:63
  242.2 2.7 %collective-permute-start.14 = (bf16[1,32,1536]{2,1,0:T(8,128)(2,1)S(1)}, bf16[1,32,1536]{2,1,0:T(8,128)(2,1)S(1)}, u32[]{:S(2)}, u32[]{:S(2)}) collective-permute-start(bf16[1,32,1536]{2,1,0:T(8,128)(2,1)S(1)} %dynamic-slice_convert_fusion.5), channel_id=1, source_target_pairs={{0,16},{4,20},{8,24},{12,28},{16,0},{20,4},{24,8},{28,12},{1,17},{... | collective-permute-start | bytes 294920 | tf_op jit(solution)/shard_map/ppermute | solution.py:63
  245.5 2.2 collective-permute-done.14
  (157 shorter events, 48.7 us)
Async XLA Ops:
  0.6 8.4 %copy-start = (bf16[1024,1536]{1,0:T(8,128)(2,1)S(1)}, bf16[1024,1536]{1,0:T(8,128)(2,1)}, u32[]{:S(2)}) copy-start(bf16[1024,1536]{1,0:T(8,128)(2,1)} %param.11) | copy-start | bytes 9437188
  0.6 32.7 %collective-permute-start.1 = (bf16[2,1024,128]{2,1,0:T(8,128)(2,1)}, bf16[2,1024,128]{2,1,0:T(8,128)(2,1)}, u32[]{:S(2)}, u32[]{:S(2)}) collective-permute-start(bf16[2,1024,128]{2,1,0:T(8,128)(2,1)} %param.13), channel_id=1, source_target_pairs={{0,8},{4,12},{8,16},{12,20},{16,24},{20,28},{24,0},{28,4},{1,9},{5... | collective-permute-start | bytes 1572872 | tf_op jit(solution)/shard_map/ppermute | solution.py:96
  3.7 31.3 %collective-permute-start.4 = (bf16[2,128,1024]{2,1,0:T(8,128)(2,1)}, bf16[2,128,1024]{2,1,0:T(8,128)(2,1)}, u32[]{:S(2)}, u32[]{:S(2)}) collective-permute-start(bf16[2,128,1024]{2,1,0:T(8,128)(2,1)} %param.14), channel_id=1, source_target_pairs={{0,8},{4,12},{8,16},{12,20},{16,24},{20,28},{24,0},{28,4},{1,9},{5... | collective-permute-start | bytes 1572872 | tf_op jit(solution)/shard_map/ppermute | solution.py:96
  24.4 1.0 copy-start.14
  24.5 1.4 copy-start.20
  24.5 1.9 copy-start.24
  24.6 1.0 copy-start.13
  25.6 3.5 %copy-start.26 = (bf16[2,128,8,64]{1,0,3,2:T(2,128)(2,1)}, bf16[2,128,8,64]{1,0,3,2:T(2,128)(2,1)S(1)}, u32[]{:S(2)}) copy-start(bf16[2,128,8,64]{1,0,3,2:T(2,128)(2,1)S(1)} %copy.58) | copy-start | bytes 786436
  27.0 0.8 copy-start.7
  29.1 15.9 %all-to-all-start = ((bf16[4,2,48,1024]{3,2,1,0:T(8,128)(2,1)}), bf16[4,2,48,1024]{3,2,1,0:T(8,128)(2,1)}, u32[]{:S(2)}, u32[]{:S(2)}) async-start(bf16[4,2,48,1024]{3,2,1,0:T(8,128)(2,1)} %bitcast.159), calls=%async_computation | async-start | bytes 1572864 | tf_op jit(solution)/shard_map/all_to_all | solution.py:134
  33.4 21.4 %collective-permute-start.2 = (bf16[2,1024,128]{2,1,0:T(8,128)(2,1)}, bf16[2,1024,128]{2,1,0:T(8,128)(2,1)}, u32[]{:S(2)}, u32[]{:S(2)}) collective-permute-start(bf16[2,1024,128]{2,1,0:T(8,128)(2,1)} %collective-permute-done.1), channel_id=1, source_target_pairs={{0,8},{4,12},{8,16},{12,20},{16,24},{20,28},{24,0},{28,4},{1,9},{5... | collective-permute-start | bytes 1572872 | tf_op jit(solution)/shard_map/ppermute | solution.py:96
  35.0 26.5 %collective-permute-start.5 = (bf16[2,128,1024]{2,1,0:T(8,128)(2,1)}, bf16[2,128,1024]{2,1,0:T(8,128)(2,1)}, u32[]{:S(2)}, u32[]{:S(2)}) collective-permute-start(bf16[2,128,1024]{2,1,0:T(8,128)(2,1)} %collective-permute-done.4), channel_id=1, source_target_pairs={{0,8},{4,12},{8,16},{12,20},{16,24},{20,28},{24,0},{28,4},{1,9},{5... | collective-permute-start | bytes 1572872 | tf_op jit(solution)/shard_map/ppermute | solution.py:96
  45.1 20.2 %all-to-all-start.2 = ((bf16[4,2,48,1024]{3,2,1,0:T(8,128)(2,1)}), bf16[4,2,48,1024]{3,2,1,0:T(8,128)(2,1)}, u32[]{:S(2)}, u32[]{:S(2)}) async-start(bf16[4,2,48,1024]{3,2,1,0:T(8,128)(2,1)} %bitcast.158), calls=%async_computation.2 | async-start | bytes 1572864 | tf_op jit(solution)/shard_map/all_to_all | solution.py:134
  49.3 7.1 %copy-start.30 = (bf16[2,128,1024]{2,1,0:T(8,128)(2,1)S(1)}, bf16[2,128,1024]{2,1,0:T(8,128)(2,1)}, u32[]{:S(2)}) copy-start(bf16[2,128,1024]{2,1,0:T(8,128)(2,1)} %param.14) | copy-start | bytes 1572868
  53.3 32.1 %collective-permute-start = (bf16[2,192,1024]{2,1,0:T(8,128)(2,1)}, bf16[2,192,1024]{2,1,0:T(8,128)(2,1)}, u32[]{:S(2)}, u32[]{:S(2)}) collective-permute-start(bf16[2,192,1024]{2,1,0:T(8,128)(2,1)} %bitcast.9), channel_id=1, source_target_pairs={{0,4},{4,0},{8,12},{12,8},{16,20},{20,16},{24,28},{28,24},{1,5},{5... | collective-permute-start | bytes 2359304 | tf_op jit(solution)/shard_map/ppermute | solution.py:136
  54.8 17.9 %collective-permute-start.3 = (bf16[2,1024,128]{2,1,0:T(8,128)(2,1)}, bf16[2,1024,128]{2,1,0:T(8,128)(2,1)}, u32[]{:S(2)}, u32[]{:S(2)}) collective-permute-start(bf16[2,1024,128]{2,1,0:T(8,128)(2,1)} %collective-permute-done.2), channel_id=1, source_target_pairs={{0,8},{4,12},{8,16},{12,20},{16,24},{20,28},{24,0},{28,4},{1,9},{5... | collective-permute-start | bytes 1572872 | tf_op jit(solution)/shard_map/ppermute | solution.py:96
  61.5 22.0 %collective-permute-start.6 = (bf16[2,128,1024]{2,1,0:T(8,128)(2,1)}, bf16[2,128,1024]{2,1,0:T(8,128)(2,1)}, u32[]{:S(2)}, u32[]{:S(2)}) collective-permute-start(bf16[2,128,1024]{2,1,0:T(8,128)(2,1)} %collective-permute-done.5), channel_id=1, source_target_pairs={{0,8},{4,12},{8,16},{12,20},{16,24},{20,28},{24,0},{28,4},{1,9},{5... | collective-permute-start | bytes 1572872 | tf_op jit(solution)/shard_map/ppermute | solution.py:96
  66.5 23.8 %copy-start.28 = (bf16[1,2,4,48,1024]{4,3,2,1,0:T(8,128)(2,1)}, bf16[1,2,4,48,1024]{4,3,2,1,0:T(8,128)(2,1)S(1)}, u32[]{:S(2)}) copy-start(bf16[1,2,4,48,1024]{4,3,2,1,0:T(8,128)(2,1)S(1)} %copy.61) | copy-start | bytes 2359300
  66.5 23.7 %collective-permute-start.8 = (bf16[2,192,1024]{2,1,0:T(8,128)(2,1)S(1)}, bf16[2,192,1024]{2,1,0:T(8,128)(2,1)S(1)}, u32[]{:S(2)}, u32[]{:S(2)}) collective-permute-start(bf16[2,192,1024]{2,1,0:T(8,128)(2,1)S(1)} %bitcast.174), channel_id=1, source_target_pairs={{0,4},{4,0},{8,12},{12,8},{16,20},{20,16},{24,28},{28,24},{1,5},{5... | collective-permute-start | bytes 2359304 | tf_op jit(solution)/shard_map/ppermute | solution.py:136
  88.4 5.5 %copy-start.22 = (f32[2,384,512]{2,1,0:T(8,128)}, f32[2,384,512]{2,1,0:T(8,128)S(1)}, u32[]{:S(2)}) copy-start(f32[2,384,512]{2,1,0:T(8,128)S(1)} %fusion.40) | copy-start | bytes 4718596
  90.3 3.7 %copy-start.33 = (bf16[2,192,1024]{2,1,0:T(8,128)(2,1)}, bf16[2,192,1024]{2,1,0:T(8,128)(2,1)S(1)}, u32[]{:S(2)}) copy-start(bf16[2,192,1024]{2,1,0:T(8,128)(2,1)S(1)} %collective-permute-done.8) | copy-start | bytes 2359300
  93.9 2.9 %copy-start.18 = (bf16[2,384,512]{2,1,0:T(8,128)(2,1)}, bf16[2,384,512]{2,1,0:T(8,128)(2,1)S(1)}, u32[]{:S(2)}) copy-start(bf16[2,384,512]{2,1,0:T(8,128)(2,1)S(1)} %fusion.6) | copy-start | bytes 2359300
  96.8 1.7 copy-start.3
  99.6 20.8 %collective-permute-start.9 = (bf16[2,192,1024]{2,1,0:T(8,128)(2,1)}, bf16[2,192,1024]{2,1,0:T(8,128)(2,1)}, u32[]{:S(2)}, u32[]{:S(2)}) collective-permute-start(bf16[2,192,1024]{2,1,0:T(8,128)(2,1)} %slice.45), channel_id=1, source_target_pairs={{0,4},{4,0},{8,12},{12,8},{16,20},{20,16},{24,28},{28,24},{1,5},{5... | collective-permute-start | bytes 2359304 | tf_op jit(solution)/shard_map/ppermute | solution.py:139
  101.1 5.7 %copy-start.29 = (bf16[1,2,4,48,1024]{4,3,2,1,0:T(8,128)(2,1)S(1)}, bf16[1,2,4,48,1024]{4,3,2,1,0:T(8,128)(2,1)}, u32[]{:S(2)}) copy-start(bf16[1,2,4,48,1024]{4,3,2,1,0:T(8,128)(2,1)} %copy-done.28) | copy-start | bytes 2359300
  101.1 5.7 %copy-start.34 = (bf16[2,192,1024]{2,1,0:T(8,128)(2,1)S(1)}, bf16[2,192,1024]{2,1,0:T(8,128)(2,1)}, u32[]{:S(2)}) copy-start(bf16[2,192,1024]{2,1,0:T(8,128)(2,1)} %copy-done.33) | copy-start | bytes 2359300
  104.4 1.9 copy-start.5
  104.4 2.6 %copy-start.23 = (f32[2,384,512]{2,1,0:T(8,128)S(1)}, f32[2,384,512]{2,1,0:T(8,128)}, u32[]{:S(2)}) copy-start(f32[2,384,512]{2,1,0:T(8,128)} %copy-done.22) | copy-start | bytes 4718596
  106.3 61.2 %collective-permute-start.7 = (bf16[2,192,1024]{2,1,0:T(8,128)(2,1)}, bf16[2,192,1024]{2,1,0:T(8,128)(2,1)}, u32[]{:S(2)}, u32[]{:S(2)}) collective-permute-start(bf16[2,192,1024]{2,1,0:T(8,128)(2,1)} %slice.46), channel_id=1, source_target_pairs={{0,4},{4,0},{8,12},{12,8},{16,20},{20,16},{24,28},{28,24},{1,5},{5... | collective-permute-start | bytes 2359304 | tf_op jit(solution)/shard_map/ppermute | solution.py:139
  106.9 13.4 %copy-start.4 = (f32[2,384,1024]{2,1,0:T(8,128)S(1)}, f32[2,384,1024]{2,1,0:T(8,128)}, u32[]{:S(2)}) copy-start(f32[2,384,1024]{2,1,0:T(8,128)} %copy-done.3) | copy-start | bytes 9437188
  108.3 13.4 %copy-start.16 = (f32[2,512,1024]{2,1,0:T(8,128)}, f32[2,512,1024]{2,1,0:T(8,128)S(1)}, u32[]{:S(2)}) copy-start(f32[2,512,1024]{2,1,0:T(8,128)S(1)} %fusion.37) | copy-start | bytes 12582916
  109.3 25.1 %collective-permute-start.23 = (bf16[2,128,1024]{2,1,0:T(8,128)(2,1)}, bf16[2,128,1024]{2,1,0:T(8,128)(2,1)}, u32[]{:S(2)}, u32[]{:S(2)}) collective-permute-start(bf16[2,128,1024]{2,1,0:T(8,128)(2,1)} %split.58), channel_id=1, source_target_pairs={{0,8},{4,12},{8,16},{12,20},{16,24},{20,28},{24,0},{28,4},{1,9},{5... | collective-permute-start | bytes 1572872 | tf_op jit(solution)/shard_map/ppermute | solution.py:104
  122.7 15.9 %all-to-all-start.3 = ((bf16[2,4,48,1024]{3,2,0,1:T(8,128)(2,1)}), bf16[2,4,48,1024]{3,2,0,1:T(8,128)(2,1)}, u32[]{:S(2)}, u32[]{:S(2)}) async-start(bf16[2,4,48,1024]{3,2,0,1:T(8,128)(2,1)} %copy.62), calls=%async_computation.3 | async-start | bytes 1572864 | tf_op jit(solution)/shard_map/all_to_all | solution.py:142
  129.8 2.0 copy-start.2
  132.9 30.5 %collective-permute-start.20 = (bf16[2,1024,128]{2,1,0:T(8,128)(2,1)}, bf16[2,1024,128]{2,1,0:T(8,128)(2,1)}, u32[]{:S(2)}, u32[]{:S(2)}) collective-permute-start(bf16[2,1024,128]{2,1,0:T(8,128)(2,1)} %split.59), channel_id=1, source_target_pairs={{0,8},{4,12},{8,16},{12,20},{16,24},{20,28},{24,0},{28,4},{1,9},{5... | collective-permute-start | bytes 1572872 | tf_op jit(solution)/shard_map/ppermute | solution.py:104
  136.8 37.3 %collective-permute-start.24 = (bf16[2,128,1024]{2,1,0:T(8,128)(2,1)}, bf16[2,128,1024]{2,1,0:T(8,128)(2,1)}, u32[]{:S(2)}, u32[]{:S(2)}) collective-permute-start(bf16[2,128,1024]{2,1,0:T(8,128)(2,1)} %fusion.34), channel_id=1, source_target_pairs={{0,8},{4,12},{8,16},{12,20},{16,24},{20,28},{24,0},{28,4},{1,9},{5... | collective-permute-start | bytes 1572872 | tf_op jit(solution)/shard_map/ppermute | solution.py:104
  138.6 2.0 copy-start.8
  138.6 2.0 copy-start.19
  138.7 3.2 %copy-start.25 = (bf16[1024,512]{1,0:T(8,128)(2,1)S(1)}, bf16[1024,512]{1,0:T(8,128)(2,1)}, u32[]{:S(2)}) copy-start(bf16[1024,512]{1,0:T(8,128)(2,1)} %param.12) | copy-start | bytes 3145732
  146.5 3.4 %copy-start.15 = (f32[2,8,128,128]{2,3,1,0:T(8,128)S(1)}, f32[2,8,128,128]{2,3,1,0:T(8,128)}, u32[]{:S(2)}) copy-start(f32[2,8,128,128]{2,3,1,0:T(8,128)} %copy-done.14) | copy-start | bytes 3145732
  146.5 3.4 %copy-start.32 = (bf16[2,128,1,8,64]{1,4,3,0,2:T(8,128)(2,1)S(1)}, bf16[2,128,1,8,64]{1,4,3,0,2:T(8,128)(2,1)}, u32[]{:S(2)}) copy-start(bf16[2,128,1,8,64]{1,4,3,0,2:T(8,128)(2,1)} %copy.92) | copy-start | bytes 786436
  149.9 1.0 copy-start.31
  151.3 1.1 copy-start.21
  152.3 1.3 copy-start.17
  152.4 1.2 copy-start.10
  159.3 2.7 %copy-start.1 = (f32[8,2,2,32,1536]{4,3,2,1,0:T(8,128)}, f32[8,2,2,32,1536]{4,3,2,1,0:T(8,128)S(1)}, u32[]{:S(2)}) copy-start(f32[8,2,2,32,1536]{4,3,2,1,0:T(8,128)S(1)} %fusion.42) | copy-start | bytes 18874372
  162.0 5.4 %copy-start.6 = (f32[2,384,1024]{2,1,0:T(8,128)S(1)}, f32[2,384,1024]{2,1,0:T(8,128)}, u32[]{:S(2)}) copy-start(f32[2,384,1024]{2,1,0:T(8,128)} %copy-done.5) | copy-start | bytes 9437188
  163.4 30.0 %collective-permute-start.10 = (bf16[8,2,32,1536]{3,2,1,0:T(8,128)(2,1)}, bf16[8,2,32,1536]{3,2,1,0:T(8,128)(2,1)}, u32[]{:S(2)}, u32[]{:S(2)}) collective-permute-start(bf16[8,2,32,1536]{3,2,1,0:T(8,128)(2,1)} %fusion.7), channel_id=1, source_target_pairs={{0,1},{1,0},{2,3},{3,2},{4,5},{5,4},{6,7},{7,6},{8,9},{9,8},{10,11... | collective-permute-start | bytes 4718600 | tf_op jit(solution)/shard_map/ppermute | solution.py:63
  165.9 16.9 %collective-permute-start.21 = (bf16[2,1024,128]{2,1,0:T(8,128)(2,1)}, bf16[2,1024,128]{2,1,0:T(8,128)(2,1)}, u32[]{:S(2)}, u32[]{:S(2)}) collective-permute-start(bf16[2,1024,128]{2,1,0:T(8,128)(2,1)} %fusion.36), channel_id=1, source_target_pairs={{0,8},{4,12},{8,16},{12,20},{16,24},{20,28},{24,0},{28,4},{1,9},{5... | collective-permute-start | bytes 1572872 | tf_op jit(solution)/shard_map/ppermute | solution.py:104
  169.8 21.0 %all-to-all-start.1 = ((bf16[2,4,48,1024]{3,2,0,1:T(8,128)(2,1)}), bf16[2,4,48,1024]{3,2,0,1:T(8,128)(2,1)}, u32[]{:S(2)}, u32[]{:S(2)}) async-start(bf16[2,4,48,1024]{3,2,0,1:T(8,128)(2,1)} %copy.60), calls=%async_computation.1 | async-start | bytes 1572864 | tf_op jit(solution)/shard_map/all_to_all | solution.py:142
  176.3 10.8 %copy-start.27 = (bf16[2,128,8,64]{1,0,3,2:T(2,128)(2,1)S(1)}, bf16[2,128,8,64]{1,0,3,2:T(2,128)(2,1)}, u32[]{:S(2)}) copy-start(bf16[2,128,8,64]{1,0,3,2:T(2,128)(2,1)} %copy-done.26) | copy-start | bytes 786436
  176.3 23.6 %collective-permute-start.25 = (bf16[2,128,1024]{2,1,0:T(8,128)(2,1)}, bf16[2,128,1024]{2,1,0:T(8,128)(2,1)}, u32[]{:S(2)}, u32[]{:S(2)}) collective-permute-start(bf16[2,128,1024]{2,1,0:T(8,128)(2,1)} %fusion.33), channel_id=1, source_target_pairs={{0,8},{4,12},{8,16},{12,20},{16,24},{20,28},{24,0},{28,4},{1,9},{5... | collective-permute-start | bytes 1572872 | tf_op jit(solution)/shard_map/ppermute | solution.py:104
  185.0 39.6 %collective-permute-start.22 = (bf16[2,1024,128]{2,1,0:T(8,128)(2,1)}, bf16[2,1024,128]{2,1,0:T(8,128)(2,1)}, u32[]{:S(2)}, u32[]{:S(2)}) collective-permute-start(bf16[2,1024,128]{2,1,0:T(8,128)(2,1)} %fusion.35), channel_id=1, source_target_pairs={{0,8},{4,12},{8,16},{12,20},{16,24},{20,28},{24,0},{28,4},{1,9},{5... | collective-permute-start | bytes 1572872 | tf_op jit(solution)/shard_map/ppermute | solution.py:104
  188.6 1.3 copy-start.11
  190.8 5.9 %collective-permute-start.15 = (bf16[8,2,32,512]{3,2,1,0:T(8,128)(2,1)}, bf16[8,2,32,512]{3,2,1,0:T(8,128)(2,1)}, u32[]{:S(2)}, u32[]{:S(2)}) collective-permute-start(bf16[8,2,32,512]{3,2,1,0:T(8,128)(2,1)} %fusion.45), channel_id=1, source_target_pairs={{0,1},{1,0},{2,3},{3,2},{4,5},{5,4},{6,7},{7,6},{8,9},{9,8},{10,11... | collective-permute-start | bytes 1572872 | tf_op jit(solution)/shard_map/ppermute | solution.py:63
  193.4 3.4 %copy-start.12 = (f32[8,2,2,32,512]{4,3,2,1,0:T(8,128)S(1)}, f32[8,2,2,32,512]{4,3,2,1,0:T(8,128)}, u32[]{:S(2)}) copy-start(f32[8,2,2,32,512]{4,3,2,1,0:T(8,128)} %copy-done.11) | copy-start | bytes 6291460
  196.5 27.3 %collective-permute-start.11 = (bf16[8,1,32,1536]{3,2,1,0:T(8,128)(2,1)S(1)}, bf16[8,1,32,1536]{3,2,1,0:T(8,128)(2,1)S(1)}, u32[]{:S(2)}, u32[]{:S(2)}) collective-permute-start(bf16[8,1,32,1536]{3,2,1,0:T(8,128)(2,1)S(1)} %dynamic-slice_convert_fusion.1), channel_id=1, source_target_pairs={{0,2},{1,3},{2,0},{3,1},{4,6},{5,7},{6,4},{7,5},{8,10},{9,11},{10,... | collective-permute-start | bytes 2359304 | tf_op jit(solution)/shard_map/ppermute | solution.py:63
  198.0 24.1 %collective-permute-start.16 = (bf16[8,1,32,512]{3,2,1,0:T(8,128)(2,1)S(1)}, bf16[8,1,32,512]{3,2,1,0:T(8,128)(2,1)S(1)}, u32[]{:S(2)}, u32[]{:S(2)}) collective-permute-start(bf16[8,1,32,512]{3,2,1,0:T(8,128)(2,1)S(1)} %dynamic-slice_convert_fusion.3), channel_id=1, source_target_pairs={{0,2},{1,3},{2,0},{3,1},{4,6},{5,7},{6,4},{7,5},{8,10},{9,11},{10,... | collective-permute-start | bytes 786440 | tf_op jit(solution)/shard_map/ppermute | solution.py:63
  222.2 6.4 %collective-permute-start.17 = (bf16[4,32,512]{2,1,0:T(8,128)(2,1)S(1)}, bf16[4,32,512]{2,1,0:T(8,128)(2,1)S(1)}, u32[]{:S(2)}, u32[]{:S(2)}) collective-permute-start(bf16[4,32,512]{2,1,0:T(8,128)(2,1)S(1)} %fusion.69), channel_id=1, source_target_pairs={{0,4},{4,0},{8,12},{12,8},{16,20},{20,16},{24,28},{28,24},{1,5},{5... | collective-permute-start | bytes 393224 | tf_op jit(solution)/shard_map/ppermute | solution.py:63
  224.1 11.8 %collective-permute-start.12 = (bf16[4,32,1536]{2,1,0:T(8,128)(2,1)S(1)}, bf16[4,32,1536]{2,1,0:T(8,128)(2,1)S(1)}, u32[]{:S(2)}, u32[]{:S(2)}) collective-permute-start(bf16[4,32,1536]{2,1,0:T(8,128)(2,1)S(1)} %fusion.48), channel_id=1, source_target_pairs={{0,4},{4,0},{8,12},{12,8},{16,20},{20,16},{24,28},{28,24},{1,5},{5... | collective-permute-start | bytes 1179656 | tf_op jit(solution)/shard_map/ppermute | solution.py:63
  228.7 7.4 %collective-permute-start.18 = (bf16[2,32,512]{2,1,0:T(8,128)(2,1)S(1)}, bf16[2,32,512]{2,1,0:T(8,128)(2,1)S(1)}, u32[]{:S(2)}, u32[]{:S(2)}) collective-permute-start(bf16[2,32,512]{2,1,0:T(8,128)(2,1)S(1)} %fusion.70), channel_id=1, source_target_pairs={{0,8},{4,12},{8,0},{12,4},{16,24},{20,28},{24,16},{28,20},{1,9},{5... | collective-permute-start | bytes 196616 | tf_op jit(solution)/shard_map/ppermute | solution.py:63
  236.0 6.1 %collective-permute-start.13 = (bf16[2,32,1536]{2,1,0:T(8,128)(2,1)S(1)}, bf16[2,32,1536]{2,1,0:T(8,128)(2,1)S(1)}, u32[]{:S(2)}, u32[]{:S(2)}) collective-permute-start(bf16[2,32,1536]{2,1,0:T(8,128)(2,1)S(1)} %fusion.64), channel_id=1, source_target_pairs={{0,8},{4,12},{8,0},{12,4},{16,24},{20,28},{24,16},{28,20},{1,9},{5... | collective-permute-start | bytes 589832 | tf_op jit(solution)/shard_map/ppermute | solution.py:63
  236.1 8.7 %collective-permute-start.19 = (bf16[1,32,512]{2,1,0:T(8,128)(2,1)S(1)}, bf16[1,32,512]{2,1,0:T(8,128)(2,1)S(1)}, u32[]{:S(2)}, u32[]{:S(2)}) collective-permute-start(bf16[1,32,512]{2,1,0:T(8,128)(2,1)S(1)} %dynamic-slice_convert_fusion.7), channel_id=1, source_target_pairs={{0,16},{4,20},{8,24},{12,28},{16,0},{20,4},{24,8},{28,12},{1,17},{... | collective-permute-start | bytes 98312 | tf_op jit(solution)/shard_map/ppermute | solution.py:63
  242.2 5.6 %collective-permute-start.14 = (bf16[1,32,1536]{2,1,0:T(8,128)(2,1)S(1)}, bf16[1,32,1536]{2,1,0:T(8,128)(2,1)S(1)}, u32[]{:S(2)}, u32[]{:S(2)}) collective-permute-start(bf16[1,32,1536]{2,1,0:T(8,128)(2,1)S(1)} %dynamic-slice_convert_fusion.5), channel_id=1, source_target_pairs={{0,16},{4,20},{8,24},{12,28},{16,0},{20,4},{24,8},{28,12},{1,17},{... | collective-permute-start | bytes 294920 | tf_op jit(solution)/shard_map/ppermute | solution.py:63
  (1 other events, 0.8 us)
where the time goes:
time: 251 us; the launch traced here: 248 us
  waiting for transfers between devices  73.1 us (29%)
  local copies, waits for them, and re-layouts  57.8 us (23%)
  starting transfers between devices  46.4 us (18%)
  matrix products  40.9 us (16%)
  other arithmetic  28.9 us (12%)
    ppermute x10, waiting for transfers between devices, halve(): came = lax.ppermute(give, axis_name, stage_perm(count, bit))  32.1 us
    unnamed x79, local copies, waits for them, and re-layouts  28.1 us
    ppermute x6, waiting for transfers between devices, ring_gather(): slots.append(lax.ppermute(slots[-1], 'dp', pairs))  14 us
    ppermute x10, starting transfers between devices, halve(): came = lax.ppermute(give, axis_name, stage_perm(count, bit))  11.6 us
    ppermute x2, waiting for transfers between devices, to_tokens(): lax.ppermute(values[:, received:].astype(jnp.bfloat16), 'dp', partner)  9.45 us
    convert_element_type x4, other arithmetic, ring_reduce(): came = lax.ppermute(total.astype(jnp.bfloat16), 'dp', pairs)  9.36 us
    all_to_all x2, starting transfers between devices, to_experts(): lax.all_to_all(store, 'expert', split_axis=0, concat_axis=2, tiled=True)  8.4 us
    all_to_all x2, starting transfers between devices, to_tokens(): lax.all_to_all(total, 'expert', split_axis=1, concat_axis=0, tiled=True)  8.38 us
  transfers between devices with their start and end apart: 30, of which 13 were waited for; matrix products, arithmetic and copies ran while one was open for 43% of the time, Pallas kernels for 0%

commit v1 on v0

--- a/solution.py
+++ b/solution.py
@@ -139,7 +139,12 @@
         other = lax.ppermute(values[:, received:].astype(jnp.bfloat16), "dp", partner)
         total = (values[:, :received] + other.astype(jnp.float32)).astype(jnp.bfloat16)
         total = total.reshape(local_experts, shards, capacity, width)
-        returned = lax.all_to_all(total, "expert", split_axis=1, concat_axis=0, tiled=True)
+        returned = jnp.concatenate(
+            lax.all_to_all(
+                jnp.stack(jnp.split(total, lax.axis_size("expert"), axis=1)), "expert", 0, 0
+            ),
+            axis=0,
+        )
         returned = returned.reshape(all_experts * capacity, width)
         return row_contract(spread, returned)
 

time: 251 us -> 237 us (0.944)
  matrix products: 40.9 us -> 34.7 us
  local copies, waits for them, and re-layouts: 57.8 us -> 52.7 us
  waiting for transfers between devices: 73.1 us -> 69.2 us
    ppermute x2, waiting for transfers between devices: 9.45 us -> 3.82 us  [to_tokens(): lax.ppermute(values[:, received:].astype(jnp.bfloat16), 'dp', partner)]
    unnamed x79 -> x69, local copies, waits for them, and re-layouts: 28.1 us -> 26.4 us
where the time goes in v1:
time: 237 us; the launch traced here: 235 us
  waiting for transfers between devices  69.2 us (29%)
  local copies, waits for them, and re-layouts  52.7 us (22%)
  starting transfers between devices  46.7 us (20%)
  matrix products  34.7 us (15%)
  other arithmetic  30.6 us (13%)
    ppermute x10, waiting for transfers between devices, halve(): came = lax.ppermute(give, axis_name, stage_perm(count, bit))  33.5 us
    unnamed x69, local copies, waits for them, and re-layouts  26.4 us
    ppermute x6, waiting for transfers between devices, ring_gather(): slots.append(lax.ppermute(slots[-1], 'dp', pairs))  16.5 us
    ppermute x10, starting transfers between devices, halve(): came = lax.ppermute(give, axis_name, stage_perm(count, bit))  12.3 us
    convert_element_type x4, other arithmetic, ring_reduce(): came = lax.ppermute(total.astype(jnp.bfloat16), 'dp', pairs)  9.4 us
    all_to_all x2, starting transfers between devices, to_experts(): lax.all_to_all(store, 'expert', split_axis=0, concat_axis=2, tiled=True)  8.42 us
    all_to_all x2, starting transfers between devices, to_tokens(): lax.all_to_all(jnp.stack(jnp.split(total, lax.axis_size('expert'), axis=1...  8.39 us
    dot_general x4, matrix products, row_contract(): lax.dot_general(left, right, (((0,), (0,)), ((), ())), preferred_element_...  8.38 us
  transfers between devices with their start and end apart: 30, of which 13 were waited for; matrix products, arithmetic and copies ran while one was open for 43% of the time, Pallas kernels for 0%

profile of v1, /device:TPU:0, one launch (start us, length us, event | category | flops | bytes accessed | tf_op | source)
XLA Modules:
  0.0 235.2 jit_solution(1812069099982817063)
XLA Ops:
  0.6 3.1 %collective-permute-start.1 = (bf16[2,1024,128]{2,1,0:T(8,128)(2,1)}, bf16[2,1024,128]{2,1,0:T(8,128)(2,1)}, u32[]{:S(2)}, u32[]{:S(2)}) collective-permute-start(bf16[2,1024,128]{2,1,0:T(8,128)(2,1)} %param.13), channel_id=1, source_target_pairs={{0,8},{4,12},{8,16},{12,20},{16,24},{20,28},{24,0},{28,4},{1,9},{5... | collective-permute-start | bytes 1572872 | tf_op jit(solution)/shard_map/ppermute | solution.py:96
  3.7 1.6 collective-permute-start.4
  9.0 3.0 %convolution_convert_fusion = bf16[256,1536]{1,0:T(8,128)(2,1)} fusion(bf16[1024,1536]{1,0:T(8,128)(2,1)S(1)} %copy-done, bf16[256,1024]{1,0:T(8,128)(2,1)} %param.8, f32[256]{0:T(256)S(1)} %fusion.71), kind=kOutput, calls=%fused_computation.2 | convolution fusion | flops 806486016 | bytes 4457472 | tf_op jit(solution)/shard_map/dot_general | solution.py:154
  12.0 3.1 %reshape.175 = bf16[2,128,3,8,64]{4,3,2,1,0:T(8,128)(2,1)} reshape(bf16[256,1536]{1,0:T(8,128)(2,1)} %convolution_convert_fusion) | data formatting | bytes 1572864 | tf_op jit(solution)/shard_map/jvp()/reshape | solution.py:40
  15.1 2.5 %fusion.80 = (bf16[2,128,1,8,64]{4,3,2,1,0:T(8,128)(2,1)}, bf16[2,128,1,8,64]{4,3,2,1,0:T(8,128)(2,1)}, bf16[2,128,1,8,64]{4,3,2,1,0:T(8,128)(2,1)}) fusion(bf16[2,128,3,8,64]{4,3,2,1,0:T(8,128)(2,1)} %reshape.175), kind=kLoop, calls=%fused_computation.174 | loop fusion | bytes 1572864 | tf_op jit(solution)/shard_map/jvp()/slice | solution.py:43
  18.9 2.0 copy.105
  20.9 2.0 copy.106
  22.9 1.4 select_reduce_fusion
  29.1 4.2 %all-to-all-start = ((bf16[4,2,48,1024]{3,2,1,0:T(8,128)(2,1)}), bf16[4,2,48,1024]{3,2,1,0:T(8,128)(2,1)}, u32[]{:S(2)}, u32[]{:S(2)}) async-start(bf16[4,2,48,1024]{3,2,1,0:T(8,128)(2,1)} %bitcast.179), calls=%async_computation | async-start | bytes 1572864 | tf_op jit(solution)/shard_map/all_to_all | solution.py:134
  33.3 1.7 collective-permute-start.2
  35.1 2.3 convolution_convert_fusion.1
  38.3 6.8 %all-to-all-done = bf16[4,2,48,1024]{3,2,1,0:T(8,128)(2,1)} async-done(((bf16[4,2,48,1024]{3,2,1,0:T(8,128)(2,1)}), bf16[4,2,48,1024]{3,2,1,0:T(8,128)(2,1)}, u32[]{:S(2)}, u32[]{:S(2)}) %all-to-all-start) | async-done | bytes 786464 | tf_op jit(solution)/shard_map/all_to_all | solution.py:134
  45.0 4.2 %all-to-all-start.2 = ((bf16[4,2,48,1024]{3,2,1,0:T(8,128)(2,1)}), bf16[4,2,48,1024]{3,2,1,0:T(8,128)(2,1)}, u32[]{:S(2)}, u32[]{:S(2)}) async-start(bf16[4,2,48,1024]{3,2,1,0:T(8,128)(2,1)} %bitcast.178), calls=%async_computation.2 | async-start | bytes 1572864 | tf_op jit(solution)/shard_map/all_to_all | solution.py:134
  49.3 2.1 copy.69
  51.4 1.5 collective-permute-start
  52.9 1.6 collective-permute-start.3
  55.3 6.2 %collective-permute-done.5 = bf16[2,128,1024]{2,1,0:T(8,128)(2,1)} collective-permute-done((bf16[2,128,1024]{2,1,0:T(8,128)(2,1)}, bf16[2,128,1024]{2,1,0:T(8,128)(2,1)}, u32[]{:S(2)}, u32[]{:S(2)}) %collective-permute-start.5) | collective-permute-done | bytes 524320 | tf_op jit(solution)/shard_map/ppermute | solution.py:96
  61.5 1.9 constant_dynamic-update-slice_fusion.2
  63.4 1.9 constant_dynamic-update-slice_fusion.6
  66.7 1.6 collective-permute-start.8
  68.2 1.9 constant_dynamic-update-slice_fusion.1
  71.2 1.5 collective-permute-done.3
  72.8 1.9 constant_dynamic-update-slice_fusion
  74.7 8.8 %collective-permute-done.6 = bf16[2,128,1024]{2,1,0:T(8,128)(2,1)} collective-permute-done((bf16[2,128,1024]{2,1,0:T(8,128)(2,1)}, bf16[2,128,1024]{2,1,0:T(8,128)(2,1)}, u32[]{:S(2)}, u32[]{:S(2)}) %collective-permute-start.6) | collective-permute-done | bytes 524320 | tf_op jit(solution)/shard_map/ppermute | solution.py:96
  84.5 3.1 %fusion.40 = f32[2,384,512]{2,1,0:T(8,128)S(1)} fusion(bf16[2,1024,512]{2,1,0:T(8,128)(2,1)} %constant_dynamic-update-slice_fusion, bf16[2,192,1024]{2,1,0:T(8,128)(2,1)} %collective-permute-done, bf16[2,192,1024]{2,1,0:T(8,128)(2,1)} %bitcast.9), kind=kOutput, calls=%fused_computation.92 | convolution fusion | flops 808452096 | bytes 5242880 | tf_op jit(solution)/shard_map/esd,edf->esf/dot_general | solution.py:160
  88.3 1.8 fusion.6
  91.3 1.6 collective-permute-start.9
  93.9 1.6 copy-done.3
  100.7 1.6 collective-permute-start.23
  102.2 2.7 %fusion.39 = f32[2,1024,512]{2,1,0:T(8,128)S(1)} fusion(bf16[2,384,512]{2,1,0:T(8,128)(2,1)S(1)} %fusion.6, bf16[2,192,1024]{2,1,0:T(8,128)(2,1)} %collective-permute-done, bf16[2,192,1024]{2,1,0:T(8,128)(2,1)} %bitcast.9), kind=kOutput, calls=%fused_computation.91 | convolution fusion | flops 808452096 | bytes 6553600 | tf_op jit(solution)/shard_map/esd,esf->edf/dot_general | solution.py:165
  104.9 2.1 copy-done.2
  108.0 3.8 %collective-permute-done.9 = bf16[2,192,1024]{2,1,0:T(8,128)(2,1)S(1)} collective-permute-done((bf16[2,192,1024]{2,1,0:T(8,128)(2,1)S(1)}, bf16[2,192,1024]{2,1,0:T(8,128)(2,1)S(1)}, u32[]{:S(2)}, u32[]{:S(2)}) %collective-permute-start.9) | collective-permute-done | bytes 786464 | tf_op jit(solution)/shard_map/ppermute | solution.py:139
  113.1 4.2 %all-to-all-start.3 = ((bf16[4,2,1,48,1024]{4,3,1,2,0:T(8,128)(2,1)}), bf16[4,2,1,48,1024]{4,3,1,2,0:T(8,128)(2,1)}, u32[]{:S(2)}, u32[]{:S(2)}) async-start(bf16[4,2,1,48,1024]{4,3,1,2,0:T(8,128)(2,1)} %pad_maximum_fusion.9), calls=%async_computation.3 | async-start | bytes 1572864 | tf_op jit(solution)/shard_map/all_to_all | solution.py:143
  117.6 2.5 %fusion.34 = bf16[2,128,1024]{2,1,0:T(8,128)(2,1)} fusion(f32[2,512,1024]{2,1,0:T(8,128)} %copy-done.16, bf16[2,128,1024]{2,1,0:T(8,128)(2,1)} %collective-permute-done.23), kind=kLoop, calls=%fused_computation.78 | loop fusion | flops 786432 | bytes 2097152 | tf_op jit(solution)/shard_map/convert_element_type | solution.py:104
  121.4 7.5 %collective-permute-done.20 = bf16[2,1024,128]{2,1,0:T(8,128)(2,1)} collective-permute-done((bf16[2,1024,128]{2,1,0:T(8,128)(2,1)}, bf16[2,1024,128]{2,1,0:T(8,128)(2,1)}, u32[]{:S(2)}, u32[]{:S(2)}) %collective-permute-start.20) | collective-permute-done | bytes 524320 | tf_op jit(solution)/shard_map/ppermute | solution.py:104
  128.9 2.3 fusion.36
  131.2 2.3 fusion.9
  133.5 2.0 fusion.32
  137.8 1.8 copy.77
  139.6 1.7 reshape.165
  141.3 1.7 fusion.14
  143.0 1.7 fusion.22
  149.9 2.1 copy.84
  151.9 2.3 fusion.42
  154.2 2.7 %copy-done.1 = f32[8,2,2,32,1536]{4,3,2,1,0:T(8,128)} copy-done((f32[8,2,2,32,1536]{4,3,2,1,0:T(8,128)}, f32[8,2,2,32,1536]{4,3,2,1,0:T(8,128)S(1)}, u32[]{:S(2)}) %copy-start.1) | copy-done | bytes 6291480
  159.3 4.2 %all-to-all-start.1 = ((bf16[4,2,1,48,1024]{4,3,1,2,0:T(8,128)(2,1)}), bf16[4,2,1,48,1024]{4,3,1,2,0:T(8,128)(2,1)}, u32[]{:S(2)}, u32[]{:S(2)}) async-start(bf16[4,2,1,48,1024]{4,3,1,2,0:T(8,128)(2,1)} %pad_maximum_fusion.8), calls=%async_computation.1 | async-start | bytes 1572864 | tf_op jit(solution)/shard_map/all_to_all | solution.py:143
  163.5 2.3 fusion.33
  165.9 2.3 fusion.35
  168.2 1.5 collective-permute-start.22
  169.7 2.0 copy.87
  171.7 1.5 fusion.50
  175.4 2.6 %fusion.11 = bf16[256,1024]{1,0:T(8,128)(2,1)} fusion(bf16[384,1024]{1,0:T(8,128)(2,1)} %bitcast.15, bf16[256,1024]{1,0:T(8,128)(2,1)} %copy-done.5, s32[256]{0:T(256)S(1)} %multiply_add_fusion.1), kind=kOutput, calls=%fused_computation.45 | convolution fusion | flops 202211328 | bytes 1836032 | tf_op jit(solution)/shard_map/dot_general | solution.py:24
  178.0 3.0 %bitcast_add_fusion = f32[8,2,32,1536]{3,2,1,0:T(8,128)S(1)} fusion(bf16[8,2,32,1536]{3,2,1,0:T(8,128)(2,1)} %collective-permute-done.10, f32[8,2,2,32,1536]{4,3,2,1,0:T(8,128)} %copy-done.1, s32[]{:T(128)S(6)} %select_n.111), kind=kLoop, calls=%fused_computation | loop fusion | flops 1572864 | bytes 7864324 | tf_op jit(solution)/shard_map/add | solution.py:64
  181.1 2.0 collective-permute-start.11
  184.6 2.5 %slice_add_fusion.2 = f32[2,128,1024]{2,1,0:T(8,128)} fusion(f32[2,512,1024]{2,1,0:T(8,128)} %copy-done.16, bf16[2,128,1024]{2,1,0:T(8,128)(2,1)} %collective-permute-done.25), kind=kLoop, calls=%fused_computation.74 | loop fusion | flops 524288 | bytes 2621440 | tf_op jit(solution)/shard_map/add | solution.py:105
  187.1 19.9 %collective-permute-done.16 = bf16[8,1,32,512]{3,2,1,0:T(8,128)(2,1)S(1)} collective-permute-done((bf16[8,1,32,512]{3,2,1,0:T(8,128)(2,1)S(1)}, bf16[8,1,32,512]{3,2,1,0:T(8,128)(2,1)S(1)}, u32[]{:S(2)}, u32[]{:S(2)}) %collective-permute-start.16) | collective-permute-done | bytes 262176 | tf_op jit(solution)/shard_map/ppermute | solution.py:63
  207.1 1.6 collective-permute-start.17
  209.6 2.4 %slice_add_fusion.5 = f32[2,1024,128]{2,1,0:T(8,128)} fusion(f32[2,1024,512]{2,1,0:T(8,128)} %copy-done.2, bf16[2,1024,128]{2,1,0:T(8,128)(2,1)} %collective-permute-done.22), kind=kLoop, calls=%fused_computation.80 | loop fusion | flops 524288 | bytes 2621440 | tf_op jit(solution)/shard_map/add | solution.py:105
  212.0 1.6 collective-permute-done.17
  213.6 3.4 %collective-permute-start.18 = (bf16[2,32,512]{2,1,0:T(8,128)(2,1)S(1)}, bf16[2,32,512]{2,1,0:T(8,128)(2,1)S(1)}, u32[]{:S(2)}, u32[]{:S(2)}) collective-permute-start(bf16[2,32,512]{2,1,0:T(8,128)(2,1)S(1)} %fusion.70), channel_id=1, source_target_pairs={{0,8},{4,12},{8,0},{12,4},{16,24},{20,28},{24,16},{28,20},{1,9},{5... | collective-permute-start | bytes 196616 | tf_op jit(solution)/shard_map/ppermute | solution.py:63
  217.1 3.8 %collective-permute-done.12 = bf16[4,32,1536]{2,1,0:T(8,128)(2,1)S(1)} collective-permute-done((bf16[4,32,1536]{2,1,0:T(8,128)(2,1)S(1)}, bf16[4,32,1536]{2,1,0:T(8,128)(2,1)S(1)}, u32[]{:S(2)}, u32[]{:S(2)}) %collective-permute-start.12) | collective-permute-done | bytes 393248 | tf_op jit(solution)/shard_map/ppermute | solution.py:63
  221.0 3.4 %collective-permute-start.13 = (bf16[2,32,1536]{2,1,0:T(8,128)(2,1)S(1)}, bf16[2,32,1536]{2,1,0:T(8,128)(2,1)S(1)}, u32[]{:S(2)}, u32[]{:S(2)}) collective-permute-start(bf16[2,32,1536]{2,1,0:T(8,128)(2,1)S(1)} %fusion.64), channel_id=1, source_target_pairs={{0,8},{4,12},{8,0},{12,4},{16,24},{20,28},{24,16},{28,20},{1,9},{5... | collective-permute-start | bytes 589832 | tf_op jit(solution)/shard_map/ppermute | solution.py:63
  224.6 4.3 %collective-permute-done.13 = bf16[2,32,1536]{2,1,0:T(8,128)(2,1)S(1)} collective-permute-done((bf16[2,32,1536]{2,1,0:T(8,128)(2,1)S(1)}, bf16[2,32,1536]{2,1,0:T(8,128)(2,1)S(1)}, u32[]{:S(2)}, u32[]{:S(2)}) %collective-permute-start.13) | collective-permute-done | bytes 196640 | tf_op jit(solution)/shard_map/ppermute | solution.py:63
  230.6 3.9 %collective-permute-done.14 = bf16[1,32,1536]{2,1,0:T(8,128)(2,1)S(1)} collective-permute-done((bf16[1,32,1536]{2,1,0:T(8,128)(2,1)S(1)}, bf16[1,32,1536]{2,1,0:T(8,128)(2,1)S(1)}, u32[]{:S(2)}, u32[]{:S(2)}) %collective-permute-start.14) | collective-permute-done | bytes 98336 | tf_op jit(solution)/shard_map/ppermute | solution.py:63
  (149 shorter events, 44.0 us)
Async XLA Ops:
  0.6 8.4 %copy-start = (bf16[1024,1536]{1,0:T(8,128)(2,1)S(1)}, bf16[1024,1536]{1,0:T(8,128)(2,1)}, u32[]{:S(2)}) copy-start(bf16[1024,1536]{1,0:T(8,128)(2,1)} %param.11) | copy-start | bytes 9437188
  0.6 32.7 %collective-permute-start.1 = (bf16[2,1024,128]{2,1,0:T(8,128)(2,1)}, bf16[2,1024,128]{2,1,0:T(8,128)(2,1)}, u32[]{:S(2)}, u32[]{:S(2)}) collective-permute-start(bf16[2,1024,128]{2,1,0:T(8,128)(2,1)} %param.13), channel_id=1, source_target_pairs={{0,8},{4,12},{8,16},{12,20},{16,24},{20,28},{24,0},{28,4},{1,9},{5... | collective-permute-start | bytes 1572872 | tf_op jit(solution)/shard_map/ppermute | solution.py:96
  3.7 31.3 %collective-permute-start.4 = (bf16[2,128,1024]{2,1,0:T(8,128)(2,1)}, bf16[2,128,1024]{2,1,0:T(8,128)(2,1)}, u32[]{:S(2)}, u32[]{:S(2)}) collective-permute-start(bf16[2,128,1024]{2,1,0:T(8,128)(2,1)} %param.14), channel_id=1, source_target_pairs={{0,8},{4,12},{8,16},{12,20},{16,24},{20,28},{24,0},{28,4},{1,9},{5... | collective-permute-start | bytes 1572872 | tf_op jit(solution)/shard_map/ppermute | solution.py:96
  24.4 1.0 copy-start.12
  24.4 1.4 copy-start.20
  24.4 1.9 copy-start.22
  24.6 1.0 copy-start.11
  25.5 3.5 %copy-start.24 = (bf16[2,128,8,64]{1,0,3,2:T(2,128)(2,1)}, bf16[2,128,8,64]{1,0,3,2:T(2,128)(2,1)S(1)}, u32[]{:S(2)}) copy-start(bf16[2,128,8,64]{1,0,3,2:T(2,128)(2,1)S(1)} %copy.68) | copy-start | bytes 786436
  26.9 0.8 copy-start.5
  29.1 15.9 %all-to-all-start = ((bf16[4,2,48,1024]{3,2,1,0:T(8,128)(2,1)}), bf16[4,2,48,1024]{3,2,1,0:T(8,128)(2,1)}, u32[]{:S(2)}, u32[]{:S(2)}) async-start(bf16[4,2,48,1024]{3,2,1,0:T(8,128)(2,1)} %bitcast.179), calls=%async_computation | async-start | bytes 1572864 | tf_op jit(solution)/shard_map/all_to_all | solution.py:134
  33.3 4.1 %copy-start.26 = (bf16[2,1024,128]{2,1,0:T(8,128)(2,1)S(1)}, bf16[2,1024,128]{2,1,0:T(8,128)(2,1)}, u32[]{:S(2)}) copy-start(bf16[2,1024,128]{2,1,0:T(8,128)(2,1)} %param.13) | copy-start | bytes 1572868
  33.3 19.5 %collective-permute-start.2 = (bf16[2,1024,128]{2,1,0:T(8,128)(2,1)}, bf16[2,1024,128]{2,1,0:T(8,128)(2,1)}, u32[]{:S(2)}, u32[]{:S(2)}) collective-permute-start(bf16[2,1024,128]{2,1,0:T(8,128)(2,1)} %collective-permute-done.1), channel_id=1, source_target_pairs={{0,8},{4,12},{8,16},{12,20},{16,24},{20,28},{24,0},{28,4},{1,9},{5... | collective-permute-start | bytes 1572872 | tf_op jit(solution)/shard_map/ppermute | solution.py:96
  35.0 26.5 %collective-permute-start.5 = (bf16[2,128,1024]{2,1,0:T(8,128)(2,1)}, bf16[2,128,1024]{2,1,0:T(8,128)(2,1)}, u32[]{:S(2)}, u32[]{:S(2)}) collective-permute-start(bf16[2,128,1024]{2,1,0:T(8,128)(2,1)} %collective-permute-done.4), channel_id=1, source_target_pairs={{0,8},{4,12},{8,16},{12,20},{16,24},{20,28},{24,0},{28,4},{1,9},{5... | collective-permute-start | bytes 1572872 | tf_op jit(solution)/shard_map/ppermute | solution.py:96
  45.0 20.3 %all-to-all-start.2 = ((bf16[4,2,48,1024]{3,2,1,0:T(8,128)(2,1)}), bf16[4,2,48,1024]{3,2,1,0:T(8,128)(2,1)}, u32[]{:S(2)}, u32[]{:S(2)}) async-start(bf16[4,2,48,1024]{3,2,1,0:T(8,128)(2,1)} %bitcast.178), calls=%async_computation.2 | async-start | bytes 1572864 | tf_op jit(solution)/shard_map/all_to_all | solution.py:134
  49.2 5.2 %copy-start.27 = (bf16[2,128,1024]{2,1,0:T(8,128)(2,1)S(1)}, bf16[2,128,1024]{2,1,0:T(8,128)(2,1)}, u32[]{:S(2)}) copy-start(bf16[2,128,1024]{2,1,0:T(8,128)(2,1)} %param.14) | copy-start | bytes 1572868
  51.4 33.1 %collective-permute-start = (bf16[2,192,1024]{2,1,0:T(8,128)(2,1)}, bf16[2,192,1024]{2,1,0:T(8,128)(2,1)}, u32[]{:S(2)}, u32[]{:S(2)}) collective-permute-start(bf16[2,192,1024]{2,1,0:T(8,128)(2,1)} %bitcast.9), channel_id=1, source_target_pairs={{0,4},{4,0},{8,12},{12,8},{16,20},{20,16},{24,28},{28,24},{1,5},{5... | collective-permute-start | bytes 2359304 | tf_op jit(solution)/shard_map/ppermute | solution.py:136
  52.9 19.9 %collective-permute-start.3 = (bf16[2,1024,128]{2,1,0:T(8,128)(2,1)}, bf16[2,1024,128]{2,1,0:T(8,128)(2,1)}, u32[]{:S(2)}, u32[]{:S(2)}) collective-permute-start(bf16[2,1024,128]{2,1,0:T(8,128)(2,1)} %collective-permute-done.2), channel_id=1, source_target_pairs={{0,8},{4,12},{8,16},{12,20},{16,24},{20,28},{24,0},{28,4},{1,9},{5... | collective-permute-start | bytes 1572872 | tf_op jit(solution)/shard_map/ppermute | solution.py:96
  61.5 21.9 %collective-permute-start.6 = (bf16[2,128,1024]{2,1,0:T(8,128)(2,1)}, bf16[2,128,1024]{2,1,0:T(8,128)(2,1)}, u32[]{:S(2)}, u32[]{:S(2)}) collective-permute-start(bf16[2,128,1024]{2,1,0:T(8,128)(2,1)} %collective-permute-done.5), channel_id=1, source_target_pairs={{0,8},{4,12},{8,16},{12,20},{16,24},{20,28},{24,0},{28,4},{1,9},{5... | collective-permute-start | bytes 1572872 | tf_op jit(solution)/shard_map/ppermute | solution.py:96
  65.3 4.8 %copy-start.15 = (bf16[2,512,1024]{2,1,0:T(8,128)(2,1)S(1)}, bf16[2,512,1024]{2,1,0:T(8,128)(2,1)}, u32[]{:S(2)}) copy-start(bf16[2,512,1024]{2,1,0:T(8,128)(2,1)} %constant_dynamic-update-slice_fusion.6) | copy-start | bytes 6291460
  66.7 21.7 %collective-permute-start.8 = (bf16[2,192,1024]{2,1,0:T(8,128)(2,1)S(1)}, bf16[2,192,1024]{2,1,0:T(8,128)(2,1)S(1)}, u32[]{:S(2)}, u32[]{:S(2)}) collective-permute-start(bf16[2,192,1024]{2,1,0:T(8,128)(2,1)S(1)} %bitcast.194), channel_id=1, source_target_pairs={{0,4},{4,0},{8,12},{12,8},{16,20},{20,16},{24,28},{28,24},{1,5},{5... | collective-permute-start | bytes 2359304 | tf_op jit(solution)/shard_map/ppermute | solution.py:136
  87.6 2.5 %copy-start.14 = (bf16[2,1024,512]{2,1,0:T(8,128)(2,1)S(1)}, bf16[2,1024,512]{2,1,0:T(8,128)(2,1)}, u32[]{:S(2)}) copy-start(bf16[2,1024,512]{2,1,0:T(8,128)(2,1)} %constant_dynamic-update-slice_fusion) | copy-start | bytes 6291460
  91.3 20.5 %collective-permute-start.9 = (bf16[2,192,1024]{2,1,0:T(8,128)(2,1)S(1)}, bf16[2,192,1024]{2,1,0:T(8,128)(2,1)S(1)}, u32[]{:S(2)}, u32[]{:S(2)}) collective-permute-start(bf16[2,192,1024]{2,1,0:T(8,128)(2,1)S(1)} %slice.45), channel_id=1, source_target_pairs={{0,4},{4,0},{8,12},{12,8},{16,20},{20,16},{24,28},{28,24},{1,5},{5... | collective-permute-start | bytes 2359304 | tf_op jit(solution)/shard_map/ppermute | solution.py:139
  93.9 1.6 copy-start.3
  96.5 34.6 %collective-permute-start.7 = (bf16[2,192,1024]{2,1,0:T(8,128)(2,1)}, bf16[2,192,1024]{2,1,0:T(8,128)(2,1)}, u32[]{:S(2)}, u32[]{:S(2)}) collective-permute-start(bf16[2,192,1024]{2,1,0:T(8,128)(2,1)} %slice.46), channel_id=1, source_target_pairs={{0,4},{4,0},{8,12},{12,8},{16,20},{20,16},{24,28},{28,24},{1,5},{5... | collective-permute-start | bytes 2359304 | tf_op jit(solution)/shard_map/ppermute | solution.py:139
  98.4 2.2 copy-start.16
  100.7 17.0 %collective-permute-start.23 = (bf16[2,128,1024]{2,1,0:T(8,128)(2,1)}, bf16[2,128,1024]{2,1,0:T(8,128)(2,1)}, u32[]{:S(2)}, u32[]{:S(2)}) collective-permute-start(bf16[2,128,1024]{2,1,0:T(8,128)(2,1)} %split.106), channel_id=1, source_target_pairs={{0,8},{4,12},{8,16},{12,20},{16,24},{20,28},{24,0},{28,4},{1,9},{5... | collective-permute-start | bytes 1572872 | tf_op jit(solution)/shard_map/ppermute | solution.py:104
  104.9 2.1 copy-start.2
  107.9 21.0 %collective-permute-start.20 = (bf16[2,1024,128]{2,1,0:T(8,128)(2,1)}, bf16[2,1024,128]{2,1,0:T(8,128)(2,1)}, u32[]{:S(2)}, u32[]{:S(2)}) collective-permute-start(bf16[2,1024,128]{2,1,0:T(8,128)(2,1)} %split.107), channel_id=1, source_target_pairs={{0,8},{4,12},{8,16},{12,20},{16,24},{20,28},{24,0},{28,4},{1,9},{5... | collective-permute-start | bytes 1572872 | tf_op jit(solution)/shard_map/ppermute | solution.py:104
  113.1 20.4 %all-to-all-start.3 = ((bf16[4,2,1,48,1024]{4,3,1,2,0:T(8,128)(2,1)}), bf16[4,2,1,48,1024]{4,3,1,2,0:T(8,128)(2,1)}, u32[]{:S(2)}, u32[]{:S(2)}) async-start(bf16[4,2,1,48,1024]{4,3,1,2,0:T(8,128)(2,1)} %pad_maximum_fusion.9), calls=%async_computation.3 | async-start | bytes 1572864 | tf_op jit(solution)/shard_map/all_to_all | solution.py:143
  117.6 13.5 %copy-start.4 = (f32[2,384,1024]{2,1,0:T(8,128)S(1)}, f32[2,384,1024]{2,1,0:T(8,128)}, u32[]{:S(2)}) copy-start(f32[2,384,1024]{2,1,0:T(8,128)} %copy-done.3) | copy-start | bytes 9437188
  120.1 43.4 %collective-permute-start.24 = (bf16[2,128,1024]{2,1,0:T(8,128)(2,1)}, bf16[2,128,1024]{2,1,0:T(8,128)(2,1)}, u32[]{:S(2)}, u32[]{:S(2)}) collective-permute-start(bf16[2,128,1024]{2,1,0:T(8,128)(2,1)} %fusion.34), channel_id=1, source_target_pairs={{0,8},{4,12},{8,16},{12,20},{16,24},{20,28},{24,0},{28,4},{1,9},{5... | collective-permute-start | bytes 1572872 | tf_op jit(solution)/shard_map/ppermute | solution.py:104
  131.2 34.7 %collective-permute-start.21 = (bf16[2,1024,128]{2,1,0:T(8,128)(2,1)}, bf16[2,1024,128]{2,1,0:T(8,128)(2,1)}, u32[]{:S(2)}, u32[]{:S(2)}) collective-permute-start(bf16[2,1024,128]{2,1,0:T(8,128)(2,1)} %fusion.36), channel_id=1, source_target_pairs={{0,8},{4,12},{8,16},{12,20},{16,24},{20,28},{24,0},{28,4},{1,9},{5... | collective-permute-start | bytes 1572872 | tf_op jit(solution)/shard_map/ppermute | solution.py:104
  133.5 2.0 copy-start.6
  133.5 2.0 copy-start.19
  133.5 3.2 %copy-start.23 = (bf16[1024,512]{1,0:T(8,128)(2,1)S(1)}, bf16[1024,512]{1,0:T(8,128)(2,1)}, u32[]{:S(2)}) copy-start(bf16[1024,512]{1,0:T(8,128)(2,1)} %param.12) | copy-start | bytes 3145732
  135.9 0.8 copy-start.7
  141.3 3.4 %copy-start.13 = (f32[2,8,128,128]{2,3,1,0:T(8,128)S(1)}, f32[2,8,128,128]{2,3,1,0:T(8,128)}, u32[]{:S(2)}) copy-start(f32[2,8,128,128]{2,3,1,0:T(8,128)} %copy-done.12) | copy-start | bytes 3145732
  141.3 3.4 %copy-start.29 = (bf16[2,128,1,8,64]{1,4,3,0,2:T(8,128)(2,1)S(1)}, bf16[2,128,1,8,64]{1,4,3,0,2:T(8,128)(2,1)}, u32[]{:S(2)}) copy-start(bf16[2,128,1,8,64]{1,4,3,0,2:T(8,128)(2,1)} %copy.106) | copy-start | bytes 786436
  144.8 1.0 copy-start.28
  146.2 1.1 copy-start.21
  147.1 1.3 copy-start.17
  147.3 1.2 copy-start.8
  154.2 2.7 %copy-start.1 = (f32[8,2,2,32,1536]{4,3,2,1,0:T(8,128)}, f32[8,2,2,32,1536]{4,3,2,1,0:T(8,128)S(1)}, u32[]{:S(2)}) copy-start(f32[8,2,2,32,1536]{4,3,2,1,0:T(8,128)S(1)} %fusion.42) | copy-start | bytes 18874372
  156.9 1.4 copy-start.18
  158.3 19.8 %collective-permute-start.10 = (bf16[8,2,32,1536]{3,2,1,0:T(8,128)(2,1)}, bf16[8,2,32,1536]{3,2,1,0:T(8,128)(2,1)}, u32[]{:S(2)}, u32[]{:S(2)}) collective-permute-start(bf16[8,2,32,1536]{3,2,1,0:T(8,128)(2,1)} %fusion.7), channel_id=1, source_target_pairs={{0,1},{1,0},{2,3},{3,2},{4,5},{5,4},{6,7},{7,6},{8,9},{9,8},{10,11... | collective-permute-start | bytes 4718600 | tf_op jit(solution)/shard_map/ppermute | solution.py:63
  159.3 16.1 %all-to-all-start.1 = ((bf16[4,2,1,48,1024]{4,3,1,2,0:T(8,128)(2,1)}), bf16[4,2,1,48,1024]{4,3,1,2,0:T(8,128)(2,1)}, u32[]{:S(2)}, u32[]{:S(2)}) async-start(bf16[4,2,1,48,1024]{4,3,1,2,0:T(8,128)(2,1)} %pad_maximum_fusion.8), calls=%async_computation.1 | async-start | bytes 1572864 | tf_op jit(solution)/shard_map/all_to_all | solution.py:143
  165.8 5.9 %copy-start.25 = (bf16[2,128,8,64]{1,0,3,2:T(2,128)(2,1)S(1)}, bf16[2,128,8,64]{1,0,3,2:T(2,128)(2,1)}, u32[]{:S(2)}) copy-start(bf16[2,128,8,64]{1,0,3,2:T(2,128)(2,1)} %copy-done.24) | copy-start | bytes 786436
  165.8 18.7 %collective-permute-start.25 = (bf16[2,128,1024]{2,1,0:T(8,128)(2,1)}, bf16[2,128,1024]{2,1,0:T(8,128)(2,1)}, u32[]{:S(2)}, u32[]{:S(2)}) collective-permute-start(bf16[2,128,1024]{2,1,0:T(8,128)(2,1)} %fusion.33), channel_id=1, source_target_pairs={{0,8},{4,12},{8,16},{12,20},{16,24},{20,28},{24,0},{28,4},{1,9},{5... | collective-permute-start | bytes 1572872 | tf_op jit(solution)/shard_map/ppermute | solution.py:104
  168.2 41.4 %collective-permute-start.22 = (bf16[2,1024,128]{2,1,0:T(8,128)(2,1)}, bf16[2,1024,128]{2,1,0:T(8,128)(2,1)}, u32[]{:S(2)}, u32[]{:S(2)}) collective-permute-start(bf16[2,1024,128]{2,1,0:T(8,128)(2,1)} %fusion.35), channel_id=1, source_target_pairs={{0,8},{4,12},{8,16},{12,20},{16,24},{20,28},{24,0},{28,4},{1,9},{5... | collective-permute-start | bytes 1572872 | tf_op jit(solution)/shard_map/ppermute | solution.py:104
  173.3 1.3 copy-start.9
  175.4 7.7 %collective-permute-start.15 = (bf16[8,2,32,512]{3,2,1,0:T(8,128)(2,1)}, bf16[8,2,32,512]{3,2,1,0:T(8,128)(2,1)}, u32[]{:S(2)}, u32[]{:S(2)}) collective-permute-start(bf16[8,2,32,512]{3,2,1,0:T(8,128)(2,1)} %fusion.45), channel_id=1, source_target_pairs={{0,1},{1,0},{2,3},{3,2},{4,5},{5,4},{6,7},{7,6},{8,9},{9,8},{10,11... | collective-permute-start | bytes 1572872 | tf_op jit(solution)/shard_map/ppermute | solution.py:63
  178.0 5.2 %copy-start.10 = (f32[8,2,2,32,512]{4,3,2,1,0:T(8,128)S(1)}, f32[8,2,2,32,512]{4,3,2,1,0:T(8,128)}, u32[]{:S(2)}) copy-start(f32[8,2,2,32,512]{4,3,2,1,0:T(8,128)} %copy-done.9) | copy-start | bytes 6291460
  181.1 27.5 %collective-permute-start.11 = (bf16[8,1,32,1536]{3,2,1,0:T(8,128)(2,1)S(1)}, bf16[8,1,32,1536]{3,2,1,0:T(8,128)(2,1)S(1)}, u32[]{:S(2)}, u32[]{:S(2)}) collective-permute-start(bf16[8,1,32,1536]{3,2,1,0:T(8,128)(2,1)S(1)} %dynamic-slice_convert_fusion.1), channel_id=1, source_target_pairs={{0,2},{1,3},{2,0},{3,1},{4,6},{5,7},{6,4},{7,5},{8,10},{9,11},{10,... | collective-permute-start | bytes 2359304 | tf_op jit(solution)/shard_map/ppermute | solution.py:63
  184.5 22.6 %collective-permute-start.16 = (bf16[8,1,32,512]{3,2,1,0:T(8,128)(2,1)S(1)}, bf16[8,1,32,512]{3,2,1,0:T(8,128)(2,1)S(1)}, u32[]{:S(2)}, u32[]{:S(2)}) collective-permute-start(bf16[8,1,32,512]{3,2,1,0:T(8,128)(2,1)S(1)} %dynamic-slice_convert_fusion.3), channel_id=1, source_target_pairs={{0,2},{1,3},{2,0},{3,1},{4,6},{5,7},{6,4},{7,5},{8,10},{9,11},{10,... | collective-permute-start | bytes 786440 | tf_op jit(solution)/shard_map/ppermute | solution.py:63
  207.1 6.4 %collective-permute-start.17 = (bf16[4,32,512]{2,1,0:T(8,128)(2,1)S(1)}, bf16[4,32,512]{2,1,0:T(8,128)(2,1)S(1)}, u32[]{:S(2)}, u32[]{:S(2)}) collective-permute-start(bf16[4,32,512]{2,1,0:T(8,128)(2,1)S(1)} %fusion.69), channel_id=1, source_target_pairs={{0,4},{4,0},{8,12},{12,8},{16,20},{20,16},{24,28},{28,24},{1,5},{5... | collective-permute-start | bytes 393224 | tf_op jit(solution)/shard_map/ppermute | solution.py:63
  209.0 11.9 %collective-permute-start.12 = (bf16[4,32,1536]{2,1,0:T(8,128)(2,1)S(1)}, bf16[4,32,1536]{2,1,0:T(8,128)(2,1)S(1)}, u32[]{:S(2)}, u32[]{:S(2)}) collective-permute-start(bf16[4,32,1536]{2,1,0:T(8,128)(2,1)S(1)} %fusion.48), channel_id=1, source_target_pairs={{0,4},{4,0},{8,12},{12,8},{16,20},{20,16},{24,28},{28,24},{1,5},{5... | collective-permute-start | bytes 1179656 | tf_op jit(solution)/shard_map/ppermute | solution.py:63
  213.6 10.8 %collective-permute-start.18 = (bf16[2,32,512]{2,1,0:T(8,128)(2,1)S(1)}, bf16[2,32,512]{2,1,0:T(8,128)(2,1)S(1)}, u32[]{:S(2)}, u32[]{:S(2)}) collective-permute-start(bf16[2,32,512]{2,1,0:T(8,128)(2,1)S(1)} %fusion.70), channel_id=1, source_target_pairs={{0,8},{4,12},{8,0},{12,4},{16,24},{20,28},{24,16},{28,20},{1,9},{5... | collective-permute-start | bytes 196616 | tf_op jit(solution)/shard_map/ppermute | solution.py:63
  221.0 7.9 %collective-permute-start.13 = (bf16[2,32,1536]{2,1,0:T(8,128)(2,1)S(1)}, bf16[2,32,1536]{2,1,0:T(8,128)(2,1)S(1)}, u32[]{:S(2)}, u32[]{:S(2)}) collective-permute-start(bf16[2,32,1536]{2,1,0:T(8,128)(2,1)S(1)} %fusion.64), channel_id=1, source_target_pairs={{0,8},{4,12},{8,0},{12,4},{16,24},{20,28},{24,16},{28,20},{1,9},{5... | collective-permute-start | bytes 589832 | tf_op jit(solution)/shard_map/ppermute | solution.py:63
  224.5 5.5 %collective-permute-start.19 = (bf16[1,32,512]{2,1,0:T(8,128)(2,1)S(1)}, bf16[1,32,512]{2,1,0:T(8,128)(2,1)S(1)}, u32[]{:S(2)}, u32[]{:S(2)}) collective-permute-start(bf16[1,32,512]{2,1,0:T(8,128)(2,1)S(1)} %dynamic-slice_convert_fusion.7), channel_id=1, source_target_pairs={{0,16},{4,20},{8,24},{12,28},{16,0},{20,4},{24,8},{28,12},{1,17},{... | collective-permute-start | bytes 98312 | tf_op jit(solution)/shard_map/ppermute | solution.py:63
  229.0 5.6 %collective-permute-start.14 = (bf16[1,32,1536]{2,1,0:T(8,128)(2,1)S(1)}, bf16[1,32,1536]{2,1,0:T(8,128)(2,1)S(1)}, u32[]{:S(2)}, u32[]{:S(2)}) collective-permute-start(bf16[1,32,1536]{2,1,0:T(8,128)(2,1)S(1)} %dynamic-slice_convert_fusion.5), channel_id=1, source_target_pairs={{0,16},{4,20},{8,24},{12,28},{16,0},{20,4},{24,8},{28,12},{1,17},{... | collective-permute-start | bytes 294920 | tf_op jit(solution)/shard_map/ppermute | solution.py:63
